TPU v7x, 32 devices: a whole 2x2x4 slice. The times are simulated.
32 devices in a mesh: row: 2 (over core), lat: 8 (over z, x), grp: 2 (over y).
Axes of the slice: x: 2, y: 2, z: 4, core: 2. Of those that a mesh axis runs over, the one named last changes fastest.
Arguments:
- stream_in: bfloat16 [192, 3584], P(('lat', 'grp'), 'row'), may hold values from -36 to 36, as said below
- pre_gain: float32 [3584], P('row'), may hold values from 0.25 to 1.75
- gate_weight: bfloat16 [3584, 14336], P('row', ('lat', 'grp')), may hold values from -0.09375 to 0.09375
- up_weight: bfloat16 [3584, 14336], P('row', ('lat', 'grp')), may hold values from -0.09375 to 0.09375
- down_weight: bfloat16 [14336, 3584], P(('lat', 'grp'), 'row'), may hold values from -0.046875 to 0.046875
- post_gain: float32 [3584], P('row'), may hold values from 0.25 to 1.75
- enc_weight: float32 [3584, 16384], P('row', ('lat', 'grp')), may hold values from -0.09375 to 0.09375
- enc_bias: float32 [16384], P(('lat', 'grp')), may hold values from -3 to 3
- dec_weight: float32 [16384, 3584], P(('lat', 'grp'), 'row'), may hold values from -0.046875 to 0.046875
- dec_bias: float32 [3584], P('row'), may hold values from -3 to 3
Outputs:
- stream_out: bfloat16 [192, 3584], P(('lat', 'grp'), 'row')
- grad_enc: float32 [3584, 16384], P('row', ('lat', 'grp'))
- grad_enc_bias: float32 [16384], P(('lat', 'grp'))
- grad_dec: float32 [16384, 3584], P(('lat', 'grp'), 'row')
- grad_dec_bias: float32 [3584], P('row')
Inputs may be any that keep to these rules, and one draw needn't show every extreme that they name: `stream_in`: Real-valued activations with scales that differ over rows and features.
All inputs are finite; a program needn't handle non-finite values.
Results may differ from a plain program's by a relative error of at most 0.013.
Values may be sent and summed in bfloat16 or wider, within the bound.
A program may use at most 128 MiB of HBM per device.

v0:
```python
import math
import jax
import jax.numpy as jnp
from jax import lax
from jax.sharding import PartitionSpec as P

D = 3584
epsilon = 1e-06
sparsity = 0.2
sharpness = 4.0


def smooth_relu(value):
    return jax.nn.softplus(sharpness * value) / sharpness


def activate(summed, hidden_width):
    return (
        jax.nn.gelu(summed[:, :hidden_width], approximate=True) * summed[:, hidden_width:]
    ).astype(jnp.bfloat16)


def body(
    stream_in,
    pre_gain,
    gate_weight,
    up_weight,
    down_weight,
    post_gain,
    enc_weight,
    enc_bias,
    dec_weight,
    dec_bias,
):
    highest = lax.Precision.HIGHEST
    stream = stream_in.astype(jnp.float32)
    hidden_width = gate_weight.shape[1]
    squares = lax.psum(jnp.sum(stream * stream, axis=1), "row")
    normed = (stream * lax.rsqrt(squares[:, None] / D + epsilon) * pre_gain).astype(jnp.bfloat16)
    joined = jnp.concatenate([gate_weight, up_weight], axis=1)
    partial_proj = jnp.dot(
        lax.all_gather(normed, ("lat", "grp"), axis=0, tiled=True),
        joined,
        preferred_element_type=jnp.float32,
    )
    shares = lax.psum_scatter(partial_proj, "row", scatter_dimension=0, tiled=True)
    hidden = lax.all_gather(activate(shares, hidden_width), "row", axis=0, tiled=True)
    output = lax.psum_scatter(
        jnp.dot(hidden, down_weight, preferred_element_type=jnp.float32),
        ("lat", "grp"),
        scatter_dimension=0,
        tiled=True,
    )
    out_squares = lax.psum(jnp.sum(output * output, axis=1), "row")
    stream_out = (
        stream + output * lax.rsqrt(out_squares[:, None] / D + epsilon) * post_gain
    ).astype(jnp.bfloat16)
    relayed = lax.all_gather(stream_out, ("lat", "grp"), axis=0, tiled=True)
    inputs = relayed.astype(jnp.float32)
    scale = 1.0 / math.sqrt(inputs.shape[0])
    encoded = jnp.dot(inputs, enc_weight, precision=highest, preferred_element_type=jnp.float32)
    preact = lax.psum(encoded, "row") + enc_bias
    latents = smooth_relu(preact)
    partial_rec = jnp.dot(
        latents, dec_weight, precision=highest, preferred_element_type=jnp.float32
    )
    recon = lax.psum(partial_rec, ("lat", "grp"))
    residual_grad = (recon + dec_bias - inputs) * scale
    grad_dec = jnp.dot(
        latents.T, residual_grad, precision=highest, preferred_element_type=jnp.float32
    )
    grad_dec_bias = jnp.sum(residual_grad, axis=0)
    back_term = jnp.dot(
        residual_grad, dec_weight.T, precision=highest, preferred_element_type=jnp.float32
    )
    latent_grad = (
        lax.psum(back_term.astype(jnp.bfloat16), "row").astype(jnp.float32) + sparsity * scale
    )
    preact_grad = latent_grad * jax.nn.sigmoid(sharpness * preact)
    grad_enc = jnp.dot(inputs.T, preact_grad, precision=highest, preferred_element_type=jnp.float32)
    grad_enc_bias = jnp.sum(preact_grad, axis=0)
    return (stream_out, grad_enc, grad_enc_bias, grad_dec, grad_dec_bias)


def solution(mesh):
    placed = (
        P(("lat", "grp"), "row"),
        P("row"),
        P("row", ("lat", "grp")),
        P("row", ("lat", "grp")),
        P(("lat", "grp"), "row"),
        P("row"),
        P("row", ("lat", "grp")),
        P(("lat", "grp")),
        P(("lat", "grp"), "row"),
        P("row"),
    )
    return jax.shard_map(
        body,
        mesh=mesh,
        in_specs=placed,
        out_specs=(
            P(("lat", "grp"), "row"),
            P("row", ("lat", "grp")),
            P(("lat", "grp")),
            P(("lat", "grp"), "row"),
            P("row"),
        ),
        check_vma=False,
    )
```

profile of v0, /device:TPU:0, one launch (start us, length us, event | category | flops | bytes accessed | tf_op | source)
XLA Modules:
  0.0 402.0 jit_solution(2031803251081122726)
XLA Ops:
  7.2 1.1 fusion.20
  8.3 2.6 psum.35
  10.9 0.9 fusion.24
  11.8 50.0 %all-gather = bf16[16,12,1792]{2,1,0:T(8,128)(2,1)} all-gather(bf16[1,12,1792]{2,1,0:T(8,128)(2,1)S(1)} %fusion.24), channel_id=1, replica_groups=mesh['row'=2,'lat'=8,'grp'=2] {'lat','grp'}, dimensions={0}, use_global_device_ids=true | all-gather | bytes 731136 | tf_op jit(solution)/shard_map/all_gather | solution.py:42
  61.9 2.1 reshape.23
  63.9 5.6 %fusion.1 = f32[192,1792]{1,0:T(8,128)} fusion(bf16[192,1792]{1,0:T(8,128)(2,1)} %reshape.23, bf16[1792,896]{1,0:T(8,128)(2,1)} %param.13, bf16[1792,896]{1,0:T(8,128)(2,1)} %param.12), kind=kOutput, calls=%fused_computation | convolution fusion | flops 1245970432 | bytes 8486912 | tf_op jit(solution)/shard_map/dot_general | solution.py:41
  69.6 4.8 %reduce-scatter.4.cloned.1.call-done = f32[96,1792]{1,0:T(8,128)} async-done(((f32[192,1792]{1,0:T(8,128)}), f32[96,1792]{1,0:T(8,128)}) %reduce-scatter.4.cloned.1.call-update) | async-done | bytes 688144 | tf_op jit(solution)/shard_map/reduce_scatter | solution.py:46
  74.4 1.2 fusion.14
  75.6 2.1 all_gather.10
  77.7 2.0 fusion.36
  79.6 52.9 %fusion = f32[16,1792]{1,0:T(8,128)S(1)} fusion(f32[192,1792]{1,0:T(8,128)} %fusion.36), kind=kCustom, calls=%all-reduce-scatter | all-reduce-scatter fusion | flops 458753 | bytes 1491456
  132.6 1.3 collective-permute-start.2
  133.9 4.5 %collective-permute-start.1 = (f32[16,1792]{1,0:T(8,128)S(1)}, f32[16,1792]{1,0:T(8,128)}, u32[]{:S(2)}, u32[]{:S(2)}) collective-permute-start(f32[16,1792]{1,0:T(8,128)S(1)} %fusion), channel_id=1, source_target_pairs={{0,2},{1,3},{2,4},{3,5},{4,6},{5,7},{6,8},{7,9},{8,10},{9,11},{10,... | collective-permute-start | bytes 344072
  138.4 2.2 collective-permute-start
  141.2 2.4 collective-permute-start.3
  144.8 0.8 collective-permute-done.3
  145.6 8.0 %concatenate.4 = f32[76,1792]{1,0:T(8,128)} concatenate(f32[12,1792]{1,0:T(8,128)} %collective-permute-done.3, f32[16,1792]{1,0:T(8,128)S(1)} %collective-permute-done.2, f32[16,1792]{1,0:T(8,128)} %collective-permute-done.1, f32[16,1792]{1,0:T(8,128)} %collective-permute-done, f32[16,1792]{1,0:T(8,128)S(1)} %fusion), dimensions={0} | concatenate | bytes 1089536
  153.6 1.0 multiply_reduce_fusion
  154.6 2.5 psum.36
  157.1 1.0 fusion.23
  158.2 47.7 %all-gather.1 = bf16[16,12,1792]{2,1,0:T(8,128)(2,1)} all-gather(bf16[1,12,1792]{2,1,0:T(8,128)(2,1)S(1)} %bitcast.14), channel_id=1, replica_groups=mesh['row'=2,'lat'=8,'grp'=2] {'lat','grp'}, dimensions={0}, use_global_device_ids=true | all-gather | bytes 731136 | tf_op jit(solution)/shard_map/all_gather | solution.py:58
  205.8 2.1 reshape.25
  207.9 7.3 %fusion.37 = f32[192,1024]{1,0:T(8,128)} fusion(bf16[192,1792]{1,0:T(8,128)(2,1)} %reshape.25, f32[1792,1024]{1,0:T(8,128)} %param.16), kind=kOutput, calls=%fused_computation.46 | convolution fusion | flops 4227858432 | bytes 8814592 | tf_op jit(solution)/shard_map/dot_general | solution.py:61
  215.5 15.0 %all-reduce.6.cloned.1.call-done = f32[192,1024]{1,0:T(8,128)} async-done(((f32[192,1024]{1,0:T(8,128)}), f32[192,1024]{1,0:T(8,128)}) %all-reduce.6.cloned.1.call-update) | async-done | bytes 786448 | tf_op jit(solution)/shard_map/psum | solution.py:62
  230.5 9.9 %fusion.17 = f32[192,1792]{1,0:T(8,128)} fusion(f32[1024,1792]{1,0:T(8,128)} %param.18, f32[192,1024]{1,0:T(8,128)} %all-reduce.6.cloned.1.call-done, f32[1024]{0:T(1024)S(1)} %copy-done.6), kind=kOutput, calls=%fused_computation.21 | convolution fusion | flops 4229627904 | bytes 9506816 | tf_op jit(solution)/shard_map/dot_general | solution.py:64
  240.7 116.4 %all-reduce.8.cloned.1.call-done = f32[192,1792]{1,0:T(8,128)} async-done(((f32[192,1792]{1,0:T(8,128)}), f32[192,1792]{1,0:T(8,128)}) %all-reduce.8.cloned.1.call-update) | async-done | bytes 1376272 | tf_op jit(solution)/shard_map/psum | solution.py:67
  357.0 12.0 %convolution_convert_fusion = bf16[192,1024]{1,0:T(8,128)(2,1)} fusion(f32[1024,1792]{1,0:T(8,128)} %param.18, bf16[192,1792]{1,0:T(8,128)(2,1)} %reshape.25, f32[192,1792]{1,0:T(8,128)} %all-reduce.8.cloned.1.call-done, f32[1792]{0:T(1024)S(1)} %copy-done.7), kind=kOutput, calls=%fused_computation.6 | convolution fusion | flops 4229431296 | bytes 9804800 | tf_op jit(solution)/shard_map/dot_general | solution.py:73
  369.0 2.5 fusion.19
  371.5 10.1 %fusion.15 = f32[1024,1792]{1,0:T(8,128)} fusion(f32[192,1024]{1,0:T(8,128)S(1)} %copy-done.3, f32[1024]{0:T(1024)S(1)} %copy-done.6, bf16[192,1792]{1,0:T(8,128)(2,1)S(1)} %copy-done.1, f32[192,1792]{1,0:T(8,128)} %all-reduce.8.cloned.1.call-done, f32[1792]{0:T(1024)S(1)} %copy-done.7), kind=kOutput, calls=%fused_computation.20 | convolution fusion | flops 4231004160 | bytes 10202112 | tf_op jit(solution)/shard_map/dot_general | solution.py:69
  381.6 5.0 %all-reduce.10.cloned.1.call-done = bf16[192,1024]{1,0:T(8,128)(2,1)} async-done(((bf16[192,1024]{1,0:T(8,128)(2,1)}), bf16[192,1024]{1,0:T(8,128)(2,1)}) %all-reduce.10.cloned.1.call-update) | async-done | bytes 393232 | tf_op jit(solution)/shard_map/psum | solution.py:77
  386.6 2.2 fusion.34
  388.8 6.7 %fusion.35 = f32[1792,1024]{1,0:T(8,128)} fusion(bf16[192,1792]{1,0:T(8,128)(2,1)S(1)} %copy-done.2, bf16[192,1024]{1,0:T(8,128)(2,1)} %all-reduce.10.cloned.1.call-done, f32[192,1024]{1,0:T(8,128)} %all-reduce.6.cloned.1.call-done, f32[1024]{0:T(1024)S(1)} %copy-done.6), kind=kOutput, calls=%fused_computation.44 | convolution fusion | flops 4229431296 | bytes 9211904 | tf_op jit(solution)/shard_map/dot_general | solution.py:80
  (35 shorter events, 1.9 us)
Async XLA Ops:
  7.2 70.5 %copy-start = (bf16[896,1792]{1,0:T(8,128)(2,1)S(1)}, bf16[896,1792]{1,0:T(8,128)(2,1)}, u32[]{:S(2)}) copy-start(bf16[896,1792]{1,0:T(8,128)(2,1)} %param.14) | copy-start | bytes 9633796
  7.2 67.2 %reduce-scatter.4.cloned.1.call-start = ((), (), s32[]{:S(2)}) async-start(), calls=%async_computation.1 | async-start | bytes 2064384 | tf_op jit(solution)/shard_map/reduce_scatter | solution.py:46
  69.6 160.9 %all-reduce.6.cloned.1.call-start = ((), (), s32[]{:S(2)}) async-start(), calls=%async_computation.2 | async-start | bytes 1572864 | tf_op jit(solution)/shard_map/psum | solution.py:62
  77.7 65.9 %copy-start.9 = (u32[32]{0:T(128)S(1)}, u32[32]{0:T(128)}, u32[]{:S(2)}) copy-start(u32[32]{0:T(128)} %constant.30) | copy-start | bytes 388
  79.6 77.5 %copy-start.4 = (bf16[12,1792]{1,0:T(8,128)(2,1)S(1)}, bf16[12,1792]{1,0:T(8,128)(2,1)}, u32[]{:S(2)}) copy-start(bf16[12,1792]{1,0:T(8,128)(2,1)} %param.10) | copy-start | bytes 129028
  79.6 77.5 %copy-start.8 = (f32[1792]{0:T(1024)S(1)}, f32[1792]{0:T(1024)}, u32[]{:S(2)}) copy-start(f32[1792]{0:T(1024)} %param.15) | copy-start | bytes 21508
  132.6 13.1 %collective-permute-start.2 = (f32[16,1792]{1,0:T(8,128)S(1)}, f32[16,1792]{1,0:T(8,128)S(1)}, u32[]{:S(2)}, u32[]{:S(2)}) collective-permute-start(f32[16,1792]{1,0:T(8,128)S(1)} %fusion), channel_id=1, source_target_pairs={{0,3},{1,4},{2,5},{3,6},{4,7},{5,8},{6,9},{7,10},{8,11},{9,12},{10... | collective-permute-start | bytes 344072
  133.9 11.8 %collective-permute-start.1 = (f32[16,1792]{1,0:T(8,128)S(1)}, f32[16,1792]{1,0:T(8,128)}, u32[]{:S(2)}, u32[]{:S(2)}) collective-permute-start(f32[16,1792]{1,0:T(8,128)S(1)} %fusion), channel_id=1, source_target_pairs={{0,2},{1,3},{2,4},{3,5},{4,6},{5,7},{6,8},{7,9},{8,10},{9,11},{10,... | collective-permute-start | bytes 344072
  138.4 7.3 %collective-permute-start = (f32[16,1792]{1,0:T(8,128)S(1)}, f32[16,1792]{1,0:T(8,128)}, u32[]{:S(2)}, u32[]{:S(2)}) collective-permute-start(f32[16,1792]{1,0:T(8,128)S(1)} %fusion), channel_id=1, source_target_pairs={{0,1},{1,2},{2,3},{3,4},{4,5},{5,6},{6,7},{7,8},{8,9},{9,10},{10,1... | collective-permute-start | bytes 344072
  141.2 4.4 %collective-permute-start.3 = (f32[12,1792]{1,0:T(8,128)}, f32[12,1792]{1,0:T(8,128)}, u32[]{:S(2)}, u32[]{:S(2)}) collective-permute-start(f32[12,1792]{1,0:T(8,128)} %slice.10), channel_id=1, source_target_pairs={{0,4},{1,5},{2,6},{3,7},{4,8},{5,9},{6,10},{7,11},{8,12},{9,13},{1... | collective-permute-start | bytes 258056
  158.1 57.1 %copy-start.5 = (bf16[12,1792]{1,0:T(8,128)(2,1)}, bf16[12,1792]{1,0:T(8,128)(2,1)S(1)}, u32[]{:S(2)}) copy-start(bf16[12,1792]{1,0:T(8,128)(2,1)S(1)} %fusion.23) | copy-start | bytes 129028
  207.9 22.6 %copy-start.6 = (f32[1024]{0:T(1024)S(1)}, f32[1024]{0:T(1024)}, u32[]{:S(2)}) copy-start(f32[1024]{0:T(1024)} %param.17) | copy-start | bytes 12292
  215.3 141.7 %copy-start.7 = (f32[1792]{0:T(1024)S(1)}, f32[1792]{0:T(1024)}, u32[]{:S(2)}) copy-start(f32[1792]{0:T(1024)} %param.19) | copy-start | bytes 21508
  215.3 141.7 %all-reduce.8.cloned.1.call-start = ((), (), s32[]{:S(2)}) async-start(), calls=%async_computation.3 | async-start | bytes 2752512 | tf_op jit(solution)/shard_map/psum | solution.py:67
  240.4 146.2 %all-reduce.10.cloned.1.call-start = ((), (), s32[]{:S(2)}) async-start(), calls=%async_computation.4 | async-start | bytes 786432 | tf_op jit(solution)/shard_map/psum | solution.py:77
  369.0 2.5 copy-start.1
  369.0 2.5 copy-start.3
  386.6 2.2 copy-start.2
Sparse Core Ops, SparseCore 0:
  69.7 4.6 reduce-scatter.3
  215.4 15.0 all-reduce.5
  240.5 116.4 all-reduce.7
  369.1 17.4 all-reduce.9
where the time goes:
time: 403 us; the launch traced here: 402 us
  blocking collectives  158 us (39%)
  waiting for transfers between devices  142 us (35%)
  matrix products  53.5 us (13%)
  between operations  14.5 us (4%)
  local copies, waits for them, and re-layouts  13.4 us (3%)
  starting transfers between devices  10.9 us (3%)
  other arithmetic  9.95 us (2%)
    psum x1, waiting for transfers between devices, body(): recon = lax.psum(partial_rec, ('lat', 'grp'))  116 us
    unnamed x1, blocking collectives  52.9 us
    all_gather x1, blocking collectives, body(): lax.all_gather(normed, ('lat', 'grp'), axis=0, tiled=True)  50 us
    all_gather x1, blocking collectives, body(): relayed = lax.all_gather(stream_out, ('lat', 'grp'), axis=0, tiled=True)  47.7 us
    psum x1, waiting for transfers between devices, body(): preact = lax.psum(encoded, 'row') + enc_bias  15 us
    unnamed x25, local copies, waits for them, and re-layouts  13.4 us
    dot_general x1, matrix products, body(): jnp.dot(residual_grad, dec_weight.T, precision=highest, preferred_element...  12 us
    unnamed x4, starting transfers between devices  10.4 us
  transfers between devices with their start and end apart: 8, of which 5 were waited for; matrix products, arithmetic and copies ran while one was open for 3% of the time, Pallas kernels for 0%

commit v1 on v0

--- a/solution.py
+++ b/solution.py
@@ -3,11 +3,37 @@
 import jax.numpy as jnp
 from jax import lax
 from jax.sharding import PartitionSpec as P
+from jax.lax import axis_index, axis_size, ppermute
 
 D = 3584
 epsilon = 1e-06
 sparsity = 0.2
 sharpness = 4.0
+
+
+def _pack_cycles(mine_x):
+    near = axis_size(("lat", "grp"))
+    d_next, right_arr, reached = (near, axis_index(("lat", "grp")), mine_x.shape[0])
+    y = range(d_next)
+    inbox = list(map(lambda dev_j: (dev_j, (dev_j + 1) % d_next), y))
+    z = range(d_next)
+    mat_out = map(lambda dev_j: (dev_j, (dev_j - 1) % d_next), z)
+    history = list(mat_out)
+    current_arr = jnp.zeros((*mine_x.shape[:0], d_next * reached, *mine_x.shape[1:]), mine_x.dtype)
+    current_arr = lax.dynamic_update_slice_in_dim(current_arr, mine_x, right_arr * reached, axis=0)
+    lower = answer = mine_x
+    w1 = d_next // 2
+    for i0 in [*range(1, w1 + 1)]:
+        lower = ppermute(lower, axis_name=("lat", "grp"), perm=inbox)
+        current_arr = lax.dynamic_update_slice_in_dim(
+            current_arr, lower, (right_arr - i0) % d_next * reached, axis=0
+        )
+        if i0 < d_next - w1:
+            answer = ppermute(answer, ("lat", "grp"), history)
+            current_arr = lax.dynamic_update_slice_in_dim(
+                current_arr, answer, (right_arr + i0) % d_next * reached, axis=0
+            )
+    return current_arr
 
 
 def smooth_relu(value):
@@ -55,7 +81,7 @@
     stream_out = (
         stream + output * lax.rsqrt(out_squares[:, None] / D + epsilon) * post_gain
     ).astype(jnp.bfloat16)
-    relayed = lax.all_gather(stream_out, ("lat", "grp"), axis=0, tiled=True)
+    relayed = _pack_cycles(stream_out)
     inputs = relayed.astype(jnp.float32)
     scale = 1.0 / math.sqrt(inputs.shape[0])
     encoded = jnp.dot(inputs, enc_weight, precision=highest, preferred_element_type=jnp.float32)

time: 403 us -> 440 us (1.092)
  blocking collectives: 158 us -> 110 us
  starting transfers between devices: 10.9 us -> 48.1 us
  local copies, waits for them, and re-layouts: 13.4 us -> 38.8 us
  waiting for transfers between devices: 142 us -> 164 us
    all_gather x1 -> x0, blocking collectives: 47.7 us -> none  [body(): relayed = lax.all_gather(stream_out, ('lat', 'grp'), axis=0, tiled=True)]
    ppermute x0 -> x15, starting transfers between devices: none -> 37.4 us  [the longest x7 34.6 us: _pack_cycles(): answer = ppermute(answer, ('lat', 'grp'), history)]
    dynamic_update_slice x0 -> x16, local copies, waits for them, and re-layouts: none -> 24.8 us  [the longest x8 12.4 us: _pack_cycles(): lax.dynamic_update_slice_in_dim(current_arr, lower, (right_arr - i0) % d_...]
    ppermute x0 -> x15, waiting for transfers between devices: none -> 16 us  [the longest x8 15.7 us: _pack_cycles(): lower = ppermute(lower, axis_name=('lat', 'grp'), perm=inbox)]
    psum x1, waiting for transfers between devices: 15 us -> 20.5 us  [body(): preact = lax.psum(encoded, 'row') + enc_bias]
    unnamed x25 -> x36, local copies, waits for them, and re-layouts: 13.4 us -> 13.1 us
  transfers between devices with their start and end apart: 8 -> 23, of which waited for: 5 -> 13; matrix products, arithmetic and copies ran while one was open for 3% -> 9% of each run, Pallas kernels for 0% -> 0%
where the time goes in v1:
time: 440 us; the launch traced here: 439 us
  waiting for transfers between devices  164 us (37%)
  blocking collectives  110 us (25%)
  matrix products  53.5 us (12%)
  starting transfers between devices  48.1 us (11%)
  local copies, waits for them, and re-layouts  38.8 us (9%)
  between operations  14.6 us (3%)
  other arithmetic  9.95 us (2%)
    psum x1, waiting for transfers between devices, body(): recon = lax.psum(partial_rec, ('lat', 'grp'))  117 us
    unnamed x1, blocking collectives  52.9 us
    all_gather x1, blocking collectives, body(): lax.all_gather(normed, ('lat', 'grp'), axis=0, tiled=True)  50 us
    ppermute x7, starting transfers between devices, _pack_cycles(): answer = ppermute(answer, ('lat', 'grp'), history)  34.6 us
    psum x1, waiting for transfers between devices, body(): preact = lax.psum(encoded, 'row') + enc_bias  20.5 us
    ppermute x8, waiting for transfers between devices, _pack_cycles(): lower = ppermute(lower, axis_name=('lat', 'grp'), perm=inbox)  15.7 us
    unnamed x36, local copies, waits for them, and re-layouts  13.1 us
    dynamic_update_slice x8, local copies, waits for them, and re-layouts, _pack_cycles(): lax.dynamic_update_slice_in_dim(current_arr, lower, (right_arr - i0) % d_...  12.4 us
  transfers between devices with their start and end apart: 23, of which 13 were waited for; matrix products, arithmetic and copies ran while one was open for 9% of the time, Pallas kernels for 0%

profile of v1, /device:TPU:0, one launch (start us, length us, event | category | flops | bytes accessed | tf_op | source)
XLA Modules:
  0.0 438.8 jit_solution(5399708950860993879)
XLA Ops:
  8.3 2.6 psum.35
  11.8 50.0 %all-gather = bf16[16,12,1792]{2,1,0:T(8,128)(2,1)} all-gather(bf16[1,12,1792]{2,1,0:T(8,128)(2,1)S(1)} %fusion.24), channel_id=1, replica_groups=mesh['row'=2,'lat'=8,'grp'=2] {'lat','grp'}, dimensions={0}, use_global_device_ids=true | all-gather | bytes 731136 | tf_op jit(solution)/shard_map/all_gather | solution.py:68
  63.9 5.6 %fusion.1 = f32[192,1792]{1,0:T(8,128)} fusion(bf16[192,1792]{1,0:T(8,128)(2,1)} %reshape.23, bf16[1792,896]{1,0:T(8,128)(2,1)} %param.13, bf16[1792,896]{1,0:T(8,128)(2,1)} %param.12), kind=kOutput, calls=%fused_computation | convolution fusion | flops 1245970432 | bytes 8486912 | tf_op jit(solution)/shard_map/dot_general | solution.py:67
  69.6 4.8 %reduce-scatter.4.cloned.1.call-done = f32[96,1792]{1,0:T(8,128)} async-done(((f32[192,1792]{1,0:T(8,128)}), f32[96,1792]{1,0:T(8,128)}) %reduce-scatter.4.cloned.1.call-update) | async-done | bytes 688144 | tf_op jit(solution)/shard_map/reduce_scatter | solution.py:72
  79.6 52.9 %fusion = f32[16,1792]{1,0:T(8,128)S(1)} fusion(f32[192,1792]{1,0:T(8,128)} %fusion.36), kind=kCustom, calls=%all-reduce-scatter | all-reduce-scatter fusion | flops 458753 | bytes 1491456
  133.9 4.5 %collective-permute-start.16 = (f32[16,1792]{1,0:T(8,128)S(1)}, f32[16,1792]{1,0:T(8,128)}, u32[]{:S(2)}, u32[]{:S(2)}) collective-permute-start(f32[16,1792]{1,0:T(8,128)S(1)} %fusion), channel_id=1, source_target_pairs={{0,2},{1,3},{2,4},{3,5},{4,6},{5,7},{6,8},{7,9},{8,10},{9,11},{10,... | collective-permute-start | bytes 344072
  138.4 2.2 collective-permute-start.15
  141.2 2.4 collective-permute-start.18
  145.6 8.0 %concatenate.4 = f32[76,1792]{1,0:T(8,128)} concatenate(f32[12,1792]{1,0:T(8,128)} %collective-permute-done.18, f32[16,1792]{1,0:T(8,128)S(1)} %collective-permute-done.17, f32[16,1792]{1,0:T(8,128)} %collective-permute-done.16, f32[16,1792]{1,0:T(8,128)} %collective-permute-done.15, f32[16,1792]{1,0:T(8,128)S(1)} %fusion), dimensions={0} | concatenate | bytes 1089536
  154.6 2.5 psum.36
  158.2 2.8 collective-permute-start
  161.0 2.8 collective-permute-start.1
  163.8 2.2 collective-permute-done
  166.4 5.3 %collective-permute-start.3 = (bf16[12,1792]{1,0:T(8,128)(2,1)S(1)}, bf16[12,1792]{1,0:T(8,128)(2,1)S(1)}, u32[]{:S(2)}, u32[]{:S(2)}) collective-permute-start(bf16[12,1792]{1,0:T(8,128)(2,1)S(1)} %collective-permute-done.1), channel_id=1, source_target_pairs={{0,15},{1,0},{2,1},{3,2},{4,3},{5,4},{6,5},{7,6},{8,7},{9,8},{10,9... | collective-permute-start | bytes 129032 | tf_op jit(solution)/shard_map/ppermute | solution.py:32
  173.8 5.6 %collective-permute-start.5 = (bf16[12,1792]{1,0:T(8,128)(2,1)S(1)}, bf16[12,1792]{1,0:T(8,128)(2,1)S(1)}, u32[]{:S(2)}, u32[]{:S(2)}) collective-permute-start(bf16[12,1792]{1,0:T(8,128)(2,1)S(1)} %collective-permute-done.3), channel_id=1, source_target_pairs={{0,15},{1,0},{2,1},{3,2},{4,3},{5,4},{6,5},{7,6},{8,7},{9,8},{10,9... | collective-permute-start | bytes 129032 | tf_op jit(solution)/shard_map/ppermute | solution.py:32
  179.4 2.2 collective-permute-done.4
  181.7 5.6 %collective-permute-start.7 = (bf16[12,1792]{1,0:T(8,128)(2,1)S(1)}, bf16[12,1792]{1,0:T(8,128)(2,1)S(1)}, u32[]{:S(2)}, u32[]{:S(2)}) collective-permute-start(bf16[12,1792]{1,0:T(8,128)(2,1)S(1)} %collective-permute-done.5), channel_id=1, source_target_pairs={{0,15},{1,0},{2,1},{3,2},{4,3},{5,4},{6,5},{7,6},{8,7},{9,8},{10,9... | collective-permute-start | bytes 129032 | tf_op jit(solution)/shard_map/ppermute | solution.py:32
  187.3 2.2 collective-permute-done.6
  190.1 5.1 %collective-permute-start.9 = (bf16[12,1792]{1,0:T(8,128)(2,1)S(1)}, bf16[12,1792]{1,0:T(8,128)(2,1)S(1)}, u32[]{:S(2)}, u32[]{:S(2)}) collective-permute-start(bf16[12,1792]{1,0:T(8,128)(2,1)S(1)} %collective-permute-done.7), channel_id=1, source_target_pairs={{0,15},{1,0},{2,1},{3,2},{4,3},{5,4},{6,5},{7,6},{8,7},{9,8},{10,9... | collective-permute-start | bytes 129032 | tf_op jit(solution)/shard_map/ppermute | solution.py:32
  197.9 5.1 %collective-permute-start.11 = (bf16[12,1792]{1,0:T(8,128)(2,1)S(1)}, bf16[12,1792]{1,0:T(8,128)(2,1)}, u32[]{:S(2)}, u32[]{:S(2)}) collective-permute-start(bf16[12,1792]{1,0:T(8,128)(2,1)S(1)} %collective-permute-done.9), channel_id=1, source_target_pairs={{0,15},{1,0},{2,1},{3,2},{4,3},{5,4},{6,5},{7,6},{8,7},{9,8},{10,9... | collective-permute-start | bytes 129032 | tf_op jit(solution)/shard_map/ppermute | solution.py:32
  203.0 2.6 collective-permute-done.10
  206.2 5.1 %collective-permute-start.13 = (bf16[12,1792]{1,0:T(8,128)(2,1)}, bf16[12,1792]{1,0:T(8,128)(2,1)}, u32[]{:S(2)}, u32[]{:S(2)}) collective-permute-start(bf16[12,1792]{1,0:T(8,128)(2,1)} %collective-permute-done.11), channel_id=1, source_target_pairs={{0,15},{1,0},{2,1},{3,2},{4,3},{5,4},{6,5},{7,6},{8,7},{9,8},{10,9... | collective-permute-start | bytes 129032 | tf_op jit(solution)/shard_map/ppermute | solution.py:32
  239.2 7.3 %fusion.37 = f32[192,1024]{1,0:T(8,128)} fusion(bf16[192,1792]{1,0:T(8,128)(2,1)} %dynamic_update_slice.63, f32[1792,1024]{1,0:T(8,128)} %param.16), kind=kOutput, calls=%fused_computation.46 | convolution fusion | flops 4227858432 | bytes 8814592 | tf_op jit(solution)/shard_map/dot_general | solution.py:87
  246.8 20.5 %all-reduce.6.cloned.1.call-done = f32[192,1024]{1,0:T(8,128)} async-done(((f32[192,1024]{1,0:T(8,128)}), f32[192,1024]{1,0:T(8,128)}) %all-reduce.6.cloned.1.call-update) | async-done | bytes 786448 | tf_op jit(solution)/shard_map/psum | solution.py:88
  267.3 9.9 %fusion.17 = f32[192,1792]{1,0:T(8,128)} fusion(f32[1024,1792]{1,0:T(8,128)} %param.18, f32[192,1024]{1,0:T(8,128)} %all-reduce.6.cloned.1.call-done, f32[1024]{0:T(1024)S(1)} %copy-done.6), kind=kOutput, calls=%fused_computation.21 | convolution fusion | flops 4229627904 | bytes 9506816 | tf_op jit(solution)/shard_map/dot_general | solution.py:90
  277.2 116.6 %all-reduce.8.cloned.1.call-done = f32[192,1792]{1,0:T(8,128)} async-done(((f32[192,1792]{1,0:T(8,128)}), f32[192,1792]{1,0:T(8,128)}) %all-reduce.8.cloned.1.call-update) | async-done | bytes 1376272 | tf_op jit(solution)/shard_map/psum | solution.py:93
  393.8 12.0 %convolution_convert_fusion = bf16[192,1024]{1,0:T(8,128)(2,1)} fusion(f32[1024,1792]{1,0:T(8,128)} %param.18, bf16[192,1792]{1,0:T(8,128)(2,1)} %dynamic_update_slice.63, f32[192,1792]{1,0:T(8,128)} %all-reduce.8.cloned.1.call-done, f32[1792]{0:T(1024)S(1)} %copy-done.7), kind=kOutput, calls=%fused_computation.6 | convolution fusion | flops 4229431296 | bytes 9804800 | tf_op jit(solution)/shard_map/dot_general | solution.py:99
  405.8 2.5 fusion.19
  408.3 10.1 %fusion.15 = f32[1024,1792]{1,0:T(8,128)} fusion(f32[192,1024]{1,0:T(8,128)S(1)} %copy-done.3, f32[1024]{0:T(1024)S(1)} %copy-done.6, bf16[192,1792]{1,0:T(8,128)(2,1)S(1)} %copy-done.1, f32[192,1792]{1,0:T(8,128)} %all-reduce.8.cloned.1.call-done, f32[1792]{0:T(1024)S(1)} %copy-done.7), kind=kOutput, calls=%fused_computation.20 | convolution fusion | flops 4231004160 | bytes 10202112 | tf_op jit(solution)/shard_map/dot_general | solution.py:95
  418.4 5.0 %all-reduce.10.cloned.1.call-done = bf16[192,1024]{1,0:T(8,128)(2,1)} async-done(((bf16[192,1024]{1,0:T(8,128)(2,1)}), bf16[192,1024]{1,0:T(8,128)(2,1)}) %all-reduce.10.cloned.1.call-update) | async-done | bytes 393232 | tf_op jit(solution)/shard_map/psum | solution.py:103
  423.4 2.2 fusion.34
  425.6 6.7 %fusion.35 = f32[1792,1024]{1,0:T(8,128)} fusion(bf16[192,1792]{1,0:T(8,128)(2,1)S(1)} %copy-done.2, bf16[192,1024]{1,0:T(8,128)(2,1)} %all-reduce.10.cloned.1.call-done, f32[192,1024]{1,0:T(8,128)} %all-reduce.6.cloned.1.call-done, f32[1024]{0:T(1024)S(1)} %copy-done.6), kind=kOutput, calls=%fused_computation.44 | convolution fusion | flops 4229431296 | bytes 9211904 | tf_op jit(solution)/shard_map/dot_general | solution.py:106
  (92 shorter events, 49.4 us)
Async XLA Ops:
  7.2 70.5 %copy-start = (bf16[896,1792]{1,0:T(8,128)(2,1)S(1)}, bf16[896,1792]{1,0:T(8,128)(2,1)}, u32[]{:S(2)}) copy-start(bf16[896,1792]{1,0:T(8,128)(2,1)} %param.14) | copy-start | bytes 9633796
  7.2 67.2 %reduce-scatter.4.cloned.1.call-start = ((), (), s32[]{:S(2)}) async-start(), calls=%async_computation.1 | async-start | bytes 2064384 | tf_op jit(solution)/shard_map/reduce_scatter | solution.py:72
  69.6 197.7 %all-reduce.6.cloned.1.call-start = ((), (), s32[]{:S(2)}) async-start(), calls=%async_computation.2 | async-start | bytes 1572864 | tf_op jit(solution)/shard_map/psum | solution.py:88
  77.7 65.9 %copy-start.15 = (u32[32]{0:T(128)S(1)}, u32[32]{0:T(128)}, u32[]{:S(2)}) copy-start(u32[32]{0:T(128)} %constant.145) | copy-start | bytes 388
  79.6 77.5 %copy-start.4 = (bf16[12,1792]{1,0:T(8,128)(2,1)S(1)}, bf16[12,1792]{1,0:T(8,128)(2,1)}, u32[]{:S(2)}) copy-start(bf16[12,1792]{1,0:T(8,128)(2,1)} %param.10) | copy-start | bytes 129028
  79.6 77.5 %copy-start.14 = (f32[1792]{0:T(1024)S(1)}, f32[1792]{0:T(1024)}, u32[]{:S(2)}) copy-start(f32[1792]{0:T(1024)} %param.15) | copy-start | bytes 21508
  132.6 13.1 %collective-permute-start.17 = (f32[16,1792]{1,0:T(8,128)S(1)}, f32[16,1792]{1,0:T(8,128)S(1)}, u32[]{:S(2)}, u32[]{:S(2)}) collective-permute-start(f32[16,1792]{1,0:T(8,128)S(1)} %fusion), channel_id=1, source_target_pairs={{0,3},{1,4},{2,5},{3,6},{4,7},{5,8},{6,9},{7,10},{8,11},{9,12},{10... | collective-permute-start | bytes 344072
  133.9 11.8 %collective-permute-start.16 = (f32[16,1792]{1,0:T(8,128)S(1)}, f32[16,1792]{1,0:T(8,128)}, u32[]{:S(2)}, u32[]{:S(2)}) collective-permute-start(f32[16,1792]{1,0:T(8,128)S(1)} %fusion), channel_id=1, source_target_pairs={{0,2},{1,3},{2,4},{3,5},{4,6},{5,7},{6,8},{7,9},{8,10},{9,11},{10,... | collective-permute-start | bytes 344072
  138.4 7.3 %collective-permute-start.15 = (f32[16,1792]{1,0:T(8,128)S(1)}, f32[16,1792]{1,0:T(8,128)}, u32[]{:S(2)}, u32[]{:S(2)}) collective-permute-start(f32[16,1792]{1,0:T(8,128)S(1)} %fusion), channel_id=1, source_target_pairs={{0,1},{1,2},{2,3},{3,4},{4,5},{5,6},{6,7},{7,8},{8,9},{9,10},{10,1... | collective-permute-start | bytes 344072
  141.2 4.4 %collective-permute-start.18 = (f32[12,1792]{1,0:T(8,128)}, f32[12,1792]{1,0:T(8,128)}, u32[]{:S(2)}, u32[]{:S(2)}) collective-permute-start(f32[12,1792]{1,0:T(8,128)} %slice.10), channel_id=1, source_target_pairs={{0,4},{1,5},{2,6},{3,7},{4,8},{5,9},{6,10},{7,11},{8,12},{9,13},{1... | collective-permute-start | bytes 258056
  158.1 88.4 %copy-start.5 = (bf16[12,1792]{1,0:T(8,128)(2,1)}, bf16[12,1792]{1,0:T(8,128)(2,1)S(1)}, u32[]{:S(2)}) copy-start(bf16[12,1792]{1,0:T(8,128)(2,1)S(1)} %fusion.23) | copy-start | bytes 129028
  158.2 7.9 %collective-permute-start = (bf16[12,1792]{1,0:T(8,128)(2,1)S(1)}, bf16[12,1792]{1,0:T(8,128)(2,1)S(1)}, u32[]{:S(2)}, u32[]{:S(2)}) collective-permute-start(bf16[12,1792]{1,0:T(8,128)(2,1)S(1)} %fusion.23), channel_id=1, source_target_pairs={{0,1},{1,2},{2,3},{3,4},{4,5},{5,6},{6,7},{7,8},{8,9},{9,10},{10,1... | collective-permute-start | bytes 129032 | tf_op jit(solution)/shard_map/ppermute | solution.py:27
  161.0 5.4 %collective-permute-start.1 = (bf16[12,1792]{1,0:T(8,128)(2,1)S(1)}, bf16[12,1792]{1,0:T(8,128)(2,1)S(1)}, u32[]{:S(2)}, u32[]{:S(2)}) collective-permute-start(bf16[12,1792]{1,0:T(8,128)(2,1)S(1)} %fusion.23), channel_id=1, source_target_pairs={{0,15},{1,0},{2,1},{3,2},{4,3},{5,4},{6,5},{7,6},{8,7},{9,8},{10,9... | collective-permute-start | bytes 129032 | tf_op jit(solution)/shard_map/ppermute | solution.py:32
  166.0 7.8 %collective-permute-start.2 = (bf16[12,1792]{1,0:T(8,128)(2,1)S(1)}, bf16[12,1792]{1,0:T(8,128)(2,1)S(1)}, u32[]{:S(2)}, u32[]{:S(2)}) collective-permute-start(bf16[12,1792]{1,0:T(8,128)(2,1)S(1)} %collective-permute-done), channel_id=1, source_target_pairs={{0,1},{1,2},{2,3},{3,4},{4,5},{5,6},{6,7},{7,8},{8,9},{9,10},{10,1... | collective-permute-start | bytes 129032 | tf_op jit(solution)/shard_map/ppermute | solution.py:27
  166.4 7.4 %collective-permute-start.3 = (bf16[12,1792]{1,0:T(8,128)(2,1)S(1)}, bf16[12,1792]{1,0:T(8,128)(2,1)S(1)}, u32[]{:S(2)}, u32[]{:S(2)}) collective-permute-start(bf16[12,1792]{1,0:T(8,128)(2,1)S(1)} %collective-permute-done.1), channel_id=1, source_target_pairs={{0,15},{1,0},{2,1},{3,2},{4,3},{5,4},{6,5},{7,6},{8,7},{9,8},{10,9... | collective-permute-start | bytes 129032 | tf_op jit(solution)/shard_map/ppermute | solution.py:32
  173.8 7.8 %collective-permute-start.4 = (bf16[12,1792]{1,0:T(8,128)(2,1)S(1)}, bf16[12,1792]{1,0:T(8,128)(2,1)S(1)}, u32[]{:S(2)}, u32[]{:S(2)}) collective-permute-start(bf16[12,1792]{1,0:T(8,128)(2,1)S(1)} %collective-permute-done.2), channel_id=1, source_target_pairs={{0,1},{1,2},{2,3},{3,4},{4,5},{5,6},{6,7},{7,8},{8,9},{9,10},{10,1... | collective-permute-start | bytes 129032 | tf_op jit(solution)/shard_map/ppermute | solution.py:27
  173.8 7.8 %collective-permute-start.5 = (bf16[12,1792]{1,0:T(8,128)(2,1)S(1)}, bf16[12,1792]{1,0:T(8,128)(2,1)S(1)}, u32[]{:S(2)}, u32[]{:S(2)}) collective-permute-start(bf16[12,1792]{1,0:T(8,128)(2,1)S(1)} %collective-permute-done.3), channel_id=1, source_target_pairs={{0,15},{1,0},{2,1},{3,2},{4,3},{5,4},{6,5},{7,6},{8,7},{9,8},{10,9... | collective-permute-start | bytes 129032 | tf_op jit(solution)/shard_map/ppermute | solution.py:32
  181.6 7.8 %collective-permute-start.6 = (bf16[12,1792]{1,0:T(8,128)(2,1)S(1)}, bf16[12,1792]{1,0:T(8,128)(2,1)S(1)}, u32[]{:S(2)}, u32[]{:S(2)}) collective-permute-start(bf16[12,1792]{1,0:T(8,128)(2,1)S(1)} %collective-permute-done.4), channel_id=1, source_target_pairs={{0,1},{1,2},{2,3},{3,4},{4,5},{5,6},{6,7},{7,8},{8,9},{9,10},{10,1... | collective-permute-start | bytes 129032 | tf_op jit(solution)/shard_map/ppermute | solution.py:27
  181.7 7.8 %copy-start.8 = (bf16[12,1792]{1,0:T(8,128)(2,1)}, bf16[12,1792]{1,0:T(8,128)(2,1)S(1)}, u32[]{:S(2)}) copy-start(bf16[12,1792]{1,0:T(8,128)(2,1)S(1)} %collective-permute-done.5) | copy-start | bytes 129028
  181.7 7.9 %collective-permute-start.7 = (bf16[12,1792]{1,0:T(8,128)(2,1)S(1)}, bf16[12,1792]{1,0:T(8,128)(2,1)S(1)}, u32[]{:S(2)}, u32[]{:S(2)}) collective-permute-start(bf16[12,1792]{1,0:T(8,128)(2,1)S(1)} %collective-permute-done.5), channel_id=1, source_target_pairs={{0,15},{1,0},{2,1},{3,2},{4,3},{5,4},{6,5},{7,6},{8,7},{9,8},{10,9... | collective-permute-start | bytes 129032 | tf_op jit(solution)/shard_map/ppermute | solution.py:32
  189.5 7.8 %collective-permute-start.8 = (bf16[12,1792]{1,0:T(8,128)(2,1)S(1)}, bf16[12,1792]{1,0:T(8,128)(2,1)S(1)}, u32[]{:S(2)}, u32[]{:S(2)}) collective-permute-start(bf16[12,1792]{1,0:T(8,128)(2,1)S(1)} %collective-permute-done.6), channel_id=1, source_target_pairs={{0,1},{1,2},{2,3},{3,4},{4,5},{5,6},{6,7},{7,8},{8,9},{9,10},{10,1... | collective-permute-start | bytes 129032 | tf_op jit(solution)/shard_map/ppermute | solution.py:27
  190.1 7.2 %collective-permute-start.9 = (bf16[12,1792]{1,0:T(8,128)(2,1)S(1)}, bf16[12,1792]{1,0:T(8,128)(2,1)S(1)}, u32[]{:S(2)}, u32[]{:S(2)}) collective-permute-start(bf16[12,1792]{1,0:T(8,128)(2,1)S(1)} %collective-permute-done.7), channel_id=1, source_target_pairs={{0,15},{1,0},{2,1},{3,2},{4,3},{5,4},{6,5},{7,6},{8,7},{9,8},{10,9... | collective-permute-start | bytes 129032 | tf_op jit(solution)/shard_map/ppermute | solution.py:32
  197.3 8.3 %collective-permute-start.10 = (bf16[12,1792]{1,0:T(8,128)(2,1)S(1)}, bf16[12,1792]{1,0:T(8,128)(2,1)S(1)}, u32[]{:S(2)}, u32[]{:S(2)}) collective-permute-start(bf16[12,1792]{1,0:T(8,128)(2,1)S(1)} %collective-permute-done.8), channel_id=1, source_target_pairs={{0,1},{1,2},{2,3},{3,4},{4,5},{5,6},{6,7},{7,8},{8,9},{9,10},{10,1... | collective-permute-start | bytes 129032 | tf_op jit(solution)/shard_map/ppermute | solution.py:27
  197.9 7.7 %copy-start.12 = (bf16[12,1792]{1,0:T(8,128)(2,1)}, bf16[12,1792]{1,0:T(8,128)(2,1)S(1)}, u32[]{:S(2)}) copy-start(bf16[12,1792]{1,0:T(8,128)(2,1)S(1)} %collective-permute-done.9) | copy-start | bytes 129028
  197.9 7.7 %collective-permute-start.11 = (bf16[12,1792]{1,0:T(8,128)(2,1)S(1)}, bf16[12,1792]{1,0:T(8,128)(2,1)}, u32[]{:S(2)}, u32[]{:S(2)}) collective-permute-start(bf16[12,1792]{1,0:T(8,128)(2,1)S(1)} %collective-permute-done.9), channel_id=1, source_target_pairs={{0,15},{1,0},{2,1},{3,2},{4,3},{5,4},{6,5},{7,6},{8,7},{9,8},{10,9... | collective-permute-start | bytes 129032 | tf_op jit(solution)/shard_map/ppermute | solution.py:32
  205.6 7.9 %collective-permute-start.12 = (bf16[12,1792]{1,0:T(8,128)(2,1)S(1)}, bf16[12,1792]{1,0:T(8,128)(2,1)}, u32[]{:S(2)}, u32[]{:S(2)}) collective-permute-start(bf16[12,1792]{1,0:T(8,128)(2,1)S(1)} %collective-permute-done.10), channel_id=1, source_target_pairs={{0,1},{1,2},{2,3},{3,4},{4,5},{5,6},{6,7},{7,8},{8,9},{9,10},{10,1... | collective-permute-start | bytes 129032 | tf_op jit(solution)/shard_map/ppermute | solution.py:27
  206.2 29.8 %collective-permute-start.13 = (bf16[12,1792]{1,0:T(8,128)(2,1)}, bf16[12,1792]{1,0:T(8,128)(2,1)}, u32[]{:S(2)}, u32[]{:S(2)}) collective-permute-start(bf16[12,1792]{1,0:T(8,128)(2,1)} %collective-permute-done.11), channel_id=1, source_target_pairs={{0,15},{1,0},{2,1},{3,2},{4,3},{5,4},{6,5},{7,6},{8,7},{9,8},{10,9... | collective-permute-start | bytes 129032 | tf_op jit(solution)/shard_map/ppermute | solution.py:32
  213.5 24.1 %collective-permute-start.14 = (bf16[12,1792]{1,0:T(8,128)(2,1)}, bf16[12,1792]{1,0:T(8,128)(2,1)}, u32[]{:S(2)}, u32[]{:S(2)}) collective-permute-start(bf16[12,1792]{1,0:T(8,128)(2,1)} %collective-permute-done.12), channel_id=1, source_target_pairs={{0,1},{1,2},{2,3},{3,4},{4,5},{5,6},{6,7},{7,8},{8,9},{9,10},{10,1... | collective-permute-start | bytes 129032 | tf_op jit(solution)/shard_map/ppermute | solution.py:27
  239.2 28.1 %copy-start.6 = (f32[1024]{0:T(1024)S(1)}, f32[1024]{0:T(1024)}, u32[]{:S(2)}) copy-start(f32[1024]{0:T(1024)} %param.17) | copy-start | bytes 12292
  246.5 147.3 %copy-start.7 = (f32[1792]{0:T(1024)S(1)}, f32[1792]{0:T(1024)}, u32[]{:S(2)}) copy-start(f32[1792]{0:T(1024)} %param.19) | copy-start | bytes 21508
  246.5 147.2 %all-reduce.8.cloned.1.call-start = ((), (), s32[]{:S(2)}) async-start(), calls=%async_computation.3 | async-start | bytes 2752512 | tf_op jit(solution)/shard_map/psum | solution.py:93
  277.2 146.2 %all-reduce.10.cloned.1.call-start = ((), (), s32[]{:S(2)}) async-start(), calls=%async_computation.4 | async-start | bytes 786432 | tf_op jit(solution)/shard_map/psum | solution.py:103
  (7 other events, 16.2 us)
Sparse Core Ops, SparseCore 0:
  69.7 4.6 reduce-scatter.3
  246.7 20.5 all-reduce.5
  277.3 116.4 all-reduce.7
  405.9 17.4 all-reduce.9
